TPU v7x, 768 devices: a whole 4x8x12 slice. The times are simulated.
768 devices in a mesh: fsdp: 12 (over z_lo, core), dp: 64 (over x, z_hi, y).
Axes of the slice: x: 4, y: 8, z: 12 (z_hi: 2, z_lo: 6; z = z_hi * 6 + z_lo), core: 2. Of those that a mesh axis runs over, the one named last changes fastest.
Arguments:
- inputs: bfloat16 [98304, 8192], P(('fsdp', 'dp')), may hold values from -6 to 6
- cotangent: bfloat16 [98304, 7680], P(('fsdp', 'dp')), may hold values from -0.15625 to 0.15625
- projection_basis: bfloat16 [8192, 128], replicated, may hold values from -0.15625 to 0.15625
- first_moment: float32 [7680, 128], P('fsdp'), may hold values from -4 to 4
- second_moment: float32 [7680, 128], P('fsdp'), may hold values from 0.01 to 4
Outputs:
- first_new: float32 [7680, 128], P('fsdp')
- second_new: float32 [7680, 128], P('fsdp')
- update: float32 [7680, 8192], P('fsdp', 'dp')
All inputs are finite; a program needn't handle non-finite values.
Results may differ from a plain program's by a relative error of at most 0.0014.
Values sent between devices are 32-bit elements; how exact they have to be, the bound alone decides.
No kernel may reach another device: no remote copies, remote signals or barrier semaphores. Data moves between devices by JAX's collectives and lax.ppermute only.
A program may use at most 32 MiB of HBM per device.

v0:
```python
import jax
import jax.numpy as jnp
from jax import lax
from jax.sharding import PartitionSpec as P

bias_first = 1.0 - 0.9**10
bias_second = 1.0 - 0.999**10


def adam_step(gradient, first_moment, second_moment):
    first_new = 0.9 * first_moment + 0.1 * gradient
    second_new = 0.999 * second_moment + 0.001 * gradient * gradient
    direction = first_new / bias_first / (jnp.sqrt(second_new / bias_second) + 1e-08)
    return (first_new, second_new, direction)


def local(inputs, cotangent, projection_basis, first_moment, second_moment):
    projected = jnp.dot(inputs, projection_basis, preferred_element_type=jnp.float32).astype(
        jnp.bfloat16
    )
    group_sum = lax.psum_scatter(
        lax.dot_general(
            cotangent, projected, (((0,), (0,)), ((), ())), preferred_element_type=jnp.float32
        ),
        "fsdp",
        scatter_dimension=0,
        tiled=True,
    )
    gradient = lax.psum(group_sum, "dp")
    first_new, second_new, direction = adam_step(gradient, first_moment, second_moment)
    col_count = projection_basis.shape[0] // lax.axis_size("dp")
    columns = lax.dynamic_slice_in_dim(
        projection_basis, lax.axis_index("dp") * col_count, col_count, 0
    )
    update = 0.25 * jnp.dot(
        direction, columns.astype(jnp.float32).T, precision=lax.Precision.HIGHEST
    )
    return (first_new, second_new, update)


def solution(mesh):
    in_specs = (
        P(("fsdp", "dp"), None),
        P(("fsdp", "dp"), None),
        P(),
        P("fsdp", None),
        P("fsdp", None),
    )
    out_specs = (P("fsdp", None), P("fsdp", None), P("fsdp", "dp"))
    return jax.shard_map(local, mesh=mesh, in_specs=in_specs, out_specs=out_specs, check_vma=False)
```

profile of v0, /device:TPU:16, one launch (start us, length us, event | category | flops | bytes accessed | tf_op | source)
XLA Modules:
  0.0 1059.3 jit_solution(8286607555663421934)
XLA Ops:
  7.2 0.0 copy-start
  7.2 0.0 reduce-scatter.2.cloned.1.call-start
  7.2 1.5 copy-done
  8.8 5.4 convolution_bitcast_fusion
  14.2 0.0 copy-start.1
  14.2 0.0 copy-start.2
  14.2 0.0 reduce-scatter.2.cloned.1.call-update
  14.2 0.0 all-reduce.2.cloned.1.call-start
  14.2 88.3 %reduce-scatter.2.cloned.1.call-done = f32[640,128]{0,1:T(8,128)} async-done(((f32[7680,128]{0,1:T(8,128)}), f32[640,128]{0,1:T(8,128)}) %reduce-scatter.2.cloned.1.call-update) | async-done | bytes 327696 | tf_op jit(solution)/shard_map/reduce_scatter | solution.py:21
  102.5 0.0 all-reduce.2.cloned.1.call-update
  102.5 0.0 copy-done.1
  102.6 0.2 copy.9
  102.7 0.0 copy-done.2
  102.7 0.2 copy.8
  102.9 945.4 %all-reduce.2.cloned.1.call-done = f32[640,128]{0,1:T(8,128)} async-done(((f32[640,128]{0,1:T(8,128)}), f32[640,128]{0,1:T(8,128)}) %all-reduce.2.cloned.1.call-update) | async-done | bytes 327696 | tf_op jit(solution)/shard_map/psum | solution.py:29
  1048.3 1.1 fusion
  1049.4 0.9 copy.10
  1050.3 0.9 copy.11
  1051.2 1.3 convolution_multiply_fusion
Async XLA Ops:
  7.2 1.6 copy-start
  7.2 95.3 %reduce-scatter.2.cloned.1.call-start = ((), (), s32[]{:S(2)}) async-start(), calls=%async_computation.1 | async-start | bytes 4259840 | tf_op jit(solution)/shard_map/reduce_scatter | solution.py:21
  14.2 88.4 %copy-start.1 = (f32[640,128]{1,0:T(8,128)S(1)}, f32[640,128]{1,0:T(8,128)}, u32[]{:S(2)}) copy-start(f32[640,128]{1,0:T(8,128)} %param.9) | copy-start | bytes 983044
  14.2 88.5 %copy-start.2 = (f32[640,128]{1,0:T(8,128)S(1)}, f32[640,128]{1,0:T(8,128)}, u32[]{:S(2)}) copy-start(f32[640,128]{1,0:T(8,128)} %param.8) | copy-start | bytes 983044
  14.2 1034.1 %all-reduce.2.cloned.1.call-start = ((), (), s32[]{:S(2)}) async-start(), calls=%async_computation.2 | async-start | bytes 655360 | tf_op jit(solution)/shard_map/psum | solution.py:29
Sparse Core Ops, SparseCore 0:
  14.3 88.1 reduce-scatter.1
  105.7 942.5 all-reduce.1
where the time goes:
time: 1060 us
  waiting for transfers between devices  1030 us (97%)
  between operations  14.1 us (1%)
    psum x1, waiting for transfers between devices, local(): gradient = lax.psum(group_sum, 'dp')  945 us
    reduce_scatter x1, waiting for transfers between devices, local(): lax.psum_scatter(lax.dot_general(cotangent, projected, (((0,), (0,)), (()...  88.3 us
  transfers between devices with their start and end apart: 2, of which 2 were waited for; matrix products, arithmetic and copies ran while one was open for 0% of the time, Pallas kernels for 0%

commit v1 on v0

v1 whole, which is shorter than its diff:
```python
import jax
import jax.numpy as jnp
from jax import lax
from jax.experimental import pallas as pl
from jax.experimental.pallas import tpu as pltpu
from jax.sharding import PartitionSpec as P

bias_first = 1.0 - 0.9**10
bias_second = 1.0 - 0.999**10

AXES = ("fsdp", "dp")
X, Y, ZH, ZL = 4, 8, 2, 6
Z = ZH * ZL
IN, OUT, RANK, TOK = 8192, 7680, 128, 128
CHUNK = OUT // (2 * ZL)
COLS = IN // (X * ZH * Y)
KT = 4


def device(x, y, z, core):
    z_hi, z_lo = z // ZL, z % ZL
    return (((z_lo * 2 + core) * X + x) * ZH + z_hi) * Y + y


CORES = (0, 1)


def pairs(size, core):
    if core == 0:
        return [(i, i + 1) for i in range(0, size, 2)]
    return [((i + 1) % size, i) for i in range(1, size, 2)]


NEAR = [
    [device(x, y, z, c) for z in pz for x in px for y in py]
    for c in CORES
    for px in pairs(X, c)
    for py in pairs(Y, c)
    for pz in pairs(Z, c)
]
FAR = [
    [device(2 * i + a, 2 * j + b, z, c) for i in range(X // 2) for j in range(Y // 2)]
    for c in CORES
    for z in range(Z)
    for a in range(2)
    for b in range(2)
]
DEEP = [
    [device(x, y, 2 * i + p, c) for i in range(Z // 2)]
    for c in CORES
    for x in range(X)
    for y in range(Y)
    for p in range(2)
]
PLANE = [
    [
        device(2 * i + a, 2 * j + b, z, c)
        for a in range(2)
        for b in range(2)
        for i in range(X // 2)
        for j in range(Y // 2)
    ]
    for c in CORES
    for z in range(Z)
]
SWAP = [
    (device(x, y, z, c), device(x, y, z, 1 - c))
    for x in range(X)
    for y in range(Y)
    for z in range(Z)
    for c in CORES
]


def exchange(blocks, groups):
    return lax.all_to_all(blocks, AXES, 0, 0, axis_index_groups=groups, tiled=True)


def half_copies(c_hbm, c, half, sems):
    def copy(i):
        cols = pl.ds(pl.multiple_of((2 * i + half) * CHUNK, 128), CHUNK)
        return pltpu.make_async_copy(c_hbm.at[:, cols], c.at[i], sems.at[i])

    return [copy(i) for i in range(ZL)]


def half_gradient(turned, c, out):
    for i in range(ZL):
        grad = jnp.dot(turned, c[i], preferred_element_type=jnp.float32)
        out[i % 2, :, i // 2] = grad.reshape(4, RANK // 4, CHUNK)


def first_kernel(place, x_hbm, b_hbm, c_hbm, out, p_out, x, b, c, xs, bs, cs):
    width = IN // KT

    def x_copy(i):
        part = pl.ds(i * width, width)
        return pltpu.make_async_copy(x_hbm.at[:, part], x.at[:, part], xs.at[i])

    def b_copy(i):
        part = pl.ds(i * width, width)
        return pltpu.make_async_copy(b_hbm.at[part, :], b.at[part, :], bs.at[i])

    for i in range(KT):
        x_copy(i).start()
        b_copy(i).start()
    c_copies = half_copies(c_hbm, c, 1 - place[0], cs)
    for copy in c_copies:
        copy.start()
    total = jnp.zeros((TOK, RANK), jnp.float32)
    for i in range(KT):
        x_copy(i).wait()
        b_copy(i).wait()
        part = pl.ds(i * width, width)
        total += jnp.dot(x[:, part], b[part, :], preferred_element_type=jnp.float32)
    turned = total.T.astype(jnp.bfloat16)
    p_out[...] = turned
    for copy in c_copies:
        copy.wait()
    half_gradient(turned, c, out)


HALF = (2, 4, ZL // 2, RANK // 4, CHUNK)
SMEM = pl.BlockSpec(memory_space=pltpu.SMEM)
VMEM = pl.BlockSpec(memory_space=pltpu.VMEM)
HBM = pl.BlockSpec(memory_space=pltpu.HBM)


def in_hbm(array):
    return pltpu.with_memory_space_constraint(array, pltpu.HBM)


def in_vmem(array):
    return pltpu.with_memory_space_constraint(array, pltpu.VMEM)


def first(place, inputs, basis, cotangent):
    return pl.pallas_call(
        first_kernel,
        out_shape=(pltpu.VMEM(HALF, jnp.float32), pltpu.VMEM((RANK, TOK), jnp.bfloat16)),
        in_specs=[SMEM, HBM, HBM, HBM],
        out_specs=(VMEM, VMEM),
        scratch_shapes=[
            pltpu.VMEM((TOK, IN), jnp.bfloat16),
            pltpu.VMEM((IN, RANK), jnp.bfloat16),
            pltpu.VMEM((ZL, TOK, CHUNK), jnp.bfloat16),
            pltpu.SemaphoreType.DMA((KT,)),
            pltpu.SemaphoreType.DMA((KT,)),
            pltpu.SemaphoreType.DMA((ZL,)),
        ],
        compiler_params=pltpu.CompilerParams(vmem_limit_bytes=24 << 20),
        name="first",
    )(place, *map(in_hbm, (inputs, basis, cotangent)))


def own_kernel(place, turned, c_hbm, basis_hbm, m_hbm, v_hbm, out, cols, m, v, c, cs, sems):
    rows = pl.ds(pl.multiple_of(place[1] * COLS, COLS), COLS)
    copies = half_copies(c_hbm, c, place[0], cs) + [
        pltpu.make_async_copy(basis_hbm.at[rows, :], cols, sems.at[0]),
        pltpu.make_async_copy(m_hbm, m, sems.at[1]),
        pltpu.make_async_copy(v_hbm, v, sems.at[2]),
    ]
    for copy in copies:
        copy.start()
    for copy in copies:
        copy.wait()
    half_gradient(turned[...], c, out)


def own(place, turned, cotangent, basis, m, v):
    return pl.pallas_call(
        own_kernel,
        out_shape=(
            pltpu.VMEM(HALF, jnp.float32),
            pltpu.VMEM((COLS, RANK), jnp.bfloat16),
            pltpu.VMEM((CHUNK, RANK), jnp.float32),
            pltpu.VMEM((CHUNK, RANK), jnp.float32),
        ),
        in_specs=[SMEM, VMEM, HBM, HBM, HBM, HBM],
        out_specs=(VMEM,) * 4,
        scratch_shapes=[
            pltpu.VMEM((ZL, TOK, CHUNK), jnp.bfloat16),
            pltpu.SemaphoreType.DMA((ZL,)),
            pltpu.SemaphoreType.DMA((3,)),
        ],
        compiler_params=pltpu.CompilerParams(vmem_limit_bytes=24 << 20),
        cost_estimate=pl.CostEstimate(
            flops=TOK * RANK * OUT, bytes_accessed=TOK * OUT + 2 * RANK * OUT, transcendentals=0
        ),
        name="own",
    )(place, in_vmem(turned), *map(in_hbm, (cotangent, basis, m, v)))


def adam_step(gradient, first_moment, second_moment):
    first_new = 0.9 * first_moment + 0.1 * gradient
    second_new = 0.999 * second_moment + 0.001 * gradient * gradient
    direction = first_new / bias_first / (jnp.sqrt(second_new / bias_second) + 1e-08)
    return (first_new, second_new, direction)


def spread_kernel(deep, out):
    part = deep[0]
    for i in range(1, deep.shape[0]):
        part += deep[i]
    for i in range(out.shape[0]):
        out[i] = part


def spread(deep):
    return pl.pallas_call(
        spread_kernel,
        out_shape=pltpu.VMEM((X * Y,) + deep.shape[1:], jnp.float32),
        in_specs=[VMEM],
        out_specs=VMEM,
        name="spread",
    )(in_vmem(deep))


def last_kernel(parts, cols, m, v, m_hbm, v_hbm, up_hbm, turned, m_out, v_out, up_out, sems):
    copies = [
        pltpu.make_async_copy(m_out, m_hbm, sems.at[0]),
        pltpu.make_async_copy(v_out, v_hbm, sems.at[1]),
        pltpu.make_async_copy(up_out, up_hbm, sems.at[2]),
    ]
    height = parts.shape[1]
    for i in range(parts.shape[0]):
        turned[i * height : (i + 1) * height, :] = parts[i]
    first_new, second_new, direction = adam_step(turned[...].T, m[...], v[...])
    m_out[...] = first_new
    v_out[...] = second_new
    copies[0].start()
    copies[1].start()
    product = jnp.zeros(up_out.shape, jnp.float32)
    pieces = []
    for _ in range(3):
        piece = direction.astype(jnp.bfloat16)
        pieces.append(piece)
        direction = direction - piece.astype(jnp.float32)
    for piece in reversed(pieces):
        product += lax.dot_general(
            piece, cols[...], (((1,), (1,)), ((), ())), preferred_element_type=jnp.float32
        )
    up_out[...] = 0.25 * product
    copies[2].start()
    for copy in copies:
        copy.wait()


def last(parts, cols, m, v):
    shape = (CHUNK, RANK)
    out = jax.ShapeDtypeStruct(shape, jnp.float32)
    up = jax.ShapeDtypeStruct((CHUNK, COLS), jnp.float32)
    return pl.pallas_call(
        last_kernel,
        out_shape=(out, out, up),
        in_specs=[VMEM] * 4,
        out_specs=(HBM,) * 3,
        scratch_shapes=[
            pltpu.VMEM((RANK, CHUNK), jnp.float32),
            pltpu.VMEM(shape, jnp.float32),
            pltpu.VMEM(shape, jnp.float32),
            pltpu.VMEM(up.shape, jnp.float32),
            pltpu.SemaphoreType.DMA((3,)),
        ],
        name="last",
    )(*map(in_vmem, (parts, cols, m, v)))


def local(inputs, cotangent, projection_basis, first_moment, second_moment):
    place = jnp.stack([lax.axis_index("fsdp") % 2, lax.axis_index("dp")]).astype(jnp.int32)
    theirs, turned = first(place, inputs, projection_basis, cotangent)
    got = lax.ppermute(theirs, AXES, SWAP)
    mine, cols, m, v = own(
        place, turned, cotangent, projection_basis, first_moment, second_moment
    )
    both = mine + got

    near = exchange(both.reshape(8, ZL // 2, RANK // 4, CHUNK), NEAR)
    near = jnp.sum(near, axis=0).reshape(ZL // 2, 8, RANK // 32, CHUNK)
    far = exchange(near.transpose(1, 0, 2, 3), FAR)
    far = jnp.sum(far, axis=0)
    deep = exchange(jnp.concatenate([far, far], axis=0), DEEP)
    whole = exchange(spread(deep), PLANE)

    return last(whole, cols, m, v)


def solution(mesh):
    in_specs = (
        P(("fsdp", "dp"), None),
        P(("fsdp", "dp"), None),
        P(),
        P("fsdp", None),
        P("fsdp", None),
    )
    out_specs = (P("fsdp", None), P("fsdp", None), P("fsdp", "dp"))
    return jax.shard_map(local, mesh=mesh, in_specs=in_specs, out_specs=out_specs, check_vma=False)
```

time: 1060 us -> 95 us (0.09)
  the two profiles are of different devices: /device:TPU:16 before, /device:TPU:2 now
where the time goes in v1:
time: 95 us; the launch traced here: 94.7 us
  blocking collectives  82.4 us (87%)
  Pallas kernels  7.81 us (8%)
  starting transfers between devices  1.92 us (2%)
  waiting for transfers between devices  1.38 us (1%)
    all_to_all x4, blocking collectives, exchange(): lax.all_to_all(blocks, AXES, 0, 0, axis_index_groups=groups, tiled=True)  82.4 us
    pallas_call x1, Pallas kernels, first(): pl.pallas_call(first_kernel, out_shape=(pltpu.VMEM(HALF, jnp.float32), pl...  3.92 us
    pallas_call x1, Pallas kernels, own(): pl.pallas_call(own_kernel, out_shape=(pltpu.VMEM(HALF, jnp.float32), pltp...  2.55 us
    ppermute x1, starting transfers between devices, local(): got = lax.ppermute(theirs, AXES, SWAP)  1.92 us
  transfers between devices with their start and end apart: 1, of which 1 were waited for; matrix products, arithmetic and copies ran while one was open for 0% of the time, Pallas kernels for 3%

profile of v1, /device:TPU:2, one launch (start us, length us, event | category | flops | bytes accessed | tf_op | source)
XLA Modules:
  0.0 94.7 jit_solution(14376183437365700205)
XLA Ops:
  0.6 0.1 pad_add_fusion.place
  0.7 3.9 %first.1 = (f32[2,4,3,32,640]{4,3,2,1,0:T(8,128)S(1)}, bf16[128,128]{1,0:T(8,128)(2,1)S(1)}) custom-call(s32[2]{0:T(128)S(1)} %pad_add_fusion.place, bf16[128,8192]{1,0:T(8,128)(2,1)} %x_hbm.1, bf16[8192,128]{1,0:T(8,128)(2,1)} %basis_hbm.1, bf16[128,7680]{1,0:T(8,128)(2,1)} %c_hbm.3), custom_call_target="tpu_custom_call" | custom-call | tf_op jit(solution)/shard_map/first/pallas_call | solution.py:138
  4.7 1.9 %collective-permute-start = (f32[2,4,3,32,640]{4,3,2,1,0:T(8,128)S(1)}, f32[2,4,3,32,640]{4,3,2,1,0:T(8,128)S(1)}, u32[]{:S(2)}, u32[]{:S(2)}) collective-permute-start(f32[2,4,3,32,640]{4,3,2,1,0:T(8,128)S(1)} %get-tuple-element.11), channel_id=1, source_target_pairs={{0,64},{64,0},{128,192},{192,128},{256,320},{320,256},{384,448},{4... | collective-permute-start | bytes 5898248 | tf_op jit(solution)/shard_map/ppermute | solution.py:272
  6.6 2.6 %own.1 = (f32[2,4,3,32,640]{4,3,2,1,0:T(8,128)S(1)}, bf16[128,128]{1,0:T(8,128)(2,1)S(1)}, f32[640,128]{1,0:T(8,128)S(1)}, f32[640,128]{1,0:T(8,128)S(1)}) custom-call(s32[2]{0:T(128)S(1)} %pad_add_fusion.place, bf16[128,128]{1,0:T(8,128)(2,1)S(1)} %get-tuple-element.9.turned, bf16[128,7680]{1,0:T(8,128)(2,1)} %c_hbm.3, bf16[8192,128]{1,0:T(8,128)(2,1)} %basis_hbm.1, ...), custom_call_target="tpu_custom_call" | custom-call | flops 125829120 | bytes 2949120 | tf_op jit(solution)/shard_map/own/pallas_call | solution.py:171
  9.1 1.4 %collective-permute-done = f32[2,4,3,32,640]{4,3,2,1,0:T(8,128)S(1)} collective-permute-done((f32[2,4,3,32,640]{4,3,2,1,0:T(8,128)S(1)}, f32[2,4,3,32,640]{4,3,2,1,0:T(8,128)S(1)}, u32[]{:S(2)}, u32[]{:S(2)}) %collective-permute-start) | collective-permute-done | bytes 1966112 | tf_op jit(solution)/shard_map/ppermute | solution.py:272
  10.5 0.2 add.8
  10.7 26.4 %all_to_all.20 = f32[8,3,32,640]{3,2,1,0:T(8,128)S(1)} all-to-all(f32[8,3,32,640]{3,2,1,0:T(8,128)S(1)} %bitcast.4), channel_id=1, replica_groups={{0,1,16,17,128,129,144,145},{256,257,272,273,384,385,400,401},{512,513,..., dimensions={0} | all-to-all | bytes 3932160 | tf_op jit(solution)/shard_map/all_to_all | solution.py:76
  37.2 0.1 reduce_sum.18
  37.3 0.1 reshape.13
  37.4 13.3 %all_to_all.21 = f32[8,3,4,640]{3,2,1,0:T(4,128)S(1)} all-to-all(f32[8,3,4,640]{3,2,1,0:T(4,128)S(1)} %copy.8), channel_id=1, replica_groups={{0,2,4,6,32,34,36,38},{1,3,5,7,33,35,37,39},{16,18,20,22,48,50,52,54},{..., dimensions={0} | all-to-all | bytes 491520 | tf_op jit(solution)/shard_map/all_to_all | solution.py:76
  50.8 24.9 %all_to_all.22.deep = f32[6,4,640]{2,1,0:T(4,128)S(1)} all-to-all(f32[6,4,640]{2,1,0:T(4,128)S(1)} %pad_maximum_fusion), channel_id=1, replica_groups={{0,256,512,8,264,520},{128,384,640,136,392,648},{1,257,513,9,265,521},{..., dimensions={0} | all-to-all | bytes 122880 | tf_op jit(solution)/shard_map/all_to_all | solution.py:76
  75.7 17.7 %all_to_all.23.parts = f32[32,4,640]{2,1,0:T(4,128)S(1)} all-to-all(f32[32,4,640]{2,1,0:T(4,128)S(1)} %spread.1), channel_id=1, replica_groups={{0,2,4,6,32,34,36,38,1,3,5,7,33,35,37,39,16,18,20,22,48,50,52,54,17,19,..., dimensions={0} | all-to-all | bytes 655360 | tf_op jit(solution)/shard_map/all_to_all | solution.py:76
  93.4 1.3 %last.1 = (f32[640,128]{1,0:T(8,128)}, f32[640,128]{1,0:T(8,128)}, f32[640,128]{1,0:T(8,128)}) custom-call(f32[32,4,640]{2,1,0:T(4,128)S(1)} %all_to_all.23.parts, bf16[128,128]{1,0:T(8,128)(2,1)S(1)} %get-tuple-element.12.cols, f32[640,128]{1,0:T(8,128)S(1)} %get-tuple-element.13.m, f32[640,128]{1,0:T(8,128)S(1)} %get-tuple-element.14.v), custom_call_target="tpu_custom_call" | custom-call | tf_op jit(solution)/shard_map/last/pallas_call | solution.py:253
  (4 shorter events, 0.1 us)
Async XLA Ops:
  4.7 5.9 %collective-permute-start = (f32[2,4,3,32,640]{4,3,2,1,0:T(8,128)S(1)}, f32[2,4,3,32,640]{4,3,2,1,0:T(8,128)S(1)}, u32[]{:S(2)}, u32[]{:S(2)}) collective-permute-start(f32[2,4,3,32,640]{4,3,2,1,0:T(8,128)S(1)} %get-tuple-element.11), channel_id=1, source_target_pairs={{0,64},{64,0},{128,192},{192,128},{256,320},{320,256},{384,448},{4... | collective-permute-start | bytes 5898248 | tf_op jit(solution)/shard_map/ppermute | solution.py:272

commit v2 on v1

--- a/solution.py
+++ b/solution.py
@@ -25,25 +25,34 @@
 CORES = (0, 1)
 
 
-def pairs(size, core):
-    if core == 0:
-        return [(i, i + 1) for i in range(0, size, 2)]
-    return [((i + 1) % size, i) for i in range(1, size, 2)]
-
+def split(size, core, first, second):
+    return tuple(tuple((i + core) % size for i in places) for places in (first, second))
+
+
+SETS_X = [split(X, c, (1, 2), (0, 3)) for c in CORES]
+SETS_Y = [split(Y, c, (1, 2, 4, 7), (0, 3, 5, 6)) for c in CORES]
+
+
+def pairs(size, core, sets):
+    both = [((i + core) % size, (i + core + 1) % size) for i in range(0, size, 2)]
+    return [pair if pair[0] in sets[0] else pair[::-1] for pair in both]
+
+
+EVEN_ODD = (tuple(range(0, Z, 2)), tuple(range(1, Z, 2)))
 
 NEAR = [
     [device(x, y, z, c) for z in pz for x in px for y in py]
     for c in CORES
-    for px in pairs(X, c)
-    for py in pairs(Y, c)
-    for pz in pairs(Z, c)
+    for px in pairs(X, c, SETS_X[c])
+    for py in pairs(Y, c, SETS_Y[c])
+    for pz in pairs(Z, c, EVEN_ODD)
 ]
 FAR = [
-    [device(2 * i + a, 2 * j + b, z, c) for i in range(X // 2) for j in range(Y // 2)]
+    [device(x, y, z, c) for x in xs for y in ys]
     for c in CORES
     for z in range(Z)
-    for a in range(2)
-    for b in range(2)
+    for xs in SETS_X[c]
+    for ys in SETS_Y[c]
 ]
 DEEP = [
     [device(x, y, 2 * i + p, c) for i in range(Z // 2)]
@@ -53,13 +62,7 @@
     for p in range(2)
 ]
 PLANE = [
-    [
-        device(2 * i + a, 2 * j + b, z, c)
-        for a in range(2)
-        for b in range(2)
-        for i in range(X // 2)
-        for j in range(Y // 2)
-    ]
+    [device(x, y, z, c) for xs in SETS_X[c] for ys in SETS_Y[c] for x in xs for y in ys]
     for c in CORES
     for z in range(Z)
 ]
@@ -90,7 +93,7 @@
         out[i % 2, :, i // 2] = grad.reshape(4, RANK // 4, CHUNK)
 
 
-def first_kernel(place, x_hbm, b_hbm, c_hbm, out, p_out, x, b, c, xs, bs, cs):
+def first_kernel(x_hbm, b_hbm, c_hbm, out, p_out, x, b, c, xs, bs, cs):
     width = IN // KT
 
     def x_copy(i):
@@ -104,7 +107,7 @@
     for i in range(KT):
         x_copy(i).start()
         b_copy(i).start()
-    c_copies = half_copies(c_hbm, c, 1 - place[0], cs)
+    c_copies = half_copies(c_hbm, c, 1 - lax.axis_index("fsdp") % 2, cs)
     for copy in c_copies:
         copy.start()
     total = jnp.zeros((TOK, RANK), jnp.float32)
@@ -121,7 +124,6 @@
 
 
 HALF = (2, 4, ZL // 2, RANK // 4, CHUNK)
-SMEM = pl.BlockSpec(memory_space=pltpu.SMEM)
 VMEM = pl.BlockSpec(memory_space=pltpu.VMEM)
 HBM = pl.BlockSpec(memory_space=pltpu.HBM)
 
@@ -134,11 +136,11 @@
     return pltpu.with_memory_space_constraint(array, pltpu.VMEM)
 
 
-def first(place, inputs, basis, cotangent):
+def first(inputs, basis, cotangent):
     return pl.pallas_call(
         first_kernel,
         out_shape=(pltpu.VMEM(HALF, jnp.float32), pltpu.VMEM((RANK, TOK), jnp.bfloat16)),
-        in_specs=[SMEM, HBM, HBM, HBM],
+        in_specs=[HBM, HBM, HBM],
         out_specs=(VMEM, VMEM),
         scratch_shapes=[
             pltpu.VMEM((TOK, IN), jnp.bfloat16),
@@ -150,12 +152,12 @@
         ],
         compiler_params=pltpu.CompilerParams(vmem_limit_bytes=24 << 20),
         name="first",
-    )(place, *map(in_hbm, (inputs, basis, cotangent)))
-
-
-def own_kernel(place, turned, c_hbm, basis_hbm, m_hbm, v_hbm, out, cols, m, v, c, cs, sems):
-    rows = pl.ds(pl.multiple_of(place[1] * COLS, COLS), COLS)
-    copies = half_copies(c_hbm, c, place[0], cs) + [
+    )(*map(in_hbm, (inputs, basis, cotangent)))
+
+
+def own_kernel(turned, c_hbm, basis_hbm, m_hbm, v_hbm, out, cols, m, v, c, cs, sems):
+    rows = pl.ds(pl.multiple_of(lax.axis_index("dp") * COLS, COLS), COLS)
+    copies = half_copies(c_hbm, c, lax.axis_index("fsdp") % 2, cs) + [
         pltpu.make_async_copy(basis_hbm.at[rows, :], cols, sems.at[0]),
         pltpu.make_async_copy(m_hbm, m, sems.at[1]),
         pltpu.make_async_copy(v_hbm, v, sems.at[2]),
@@ -167,7 +169,7 @@
     half_gradient(turned[...], c, out)
 
 
-def own(place, turned, cotangent, basis, m, v):
+def own(turned, cotangent, basis, m, v):
     return pl.pallas_call(
         own_kernel,
         out_shape=(
@@ -176,7 +178,7 @@
             pltpu.VMEM((CHUNK, RANK), jnp.float32),
             pltpu.VMEM((CHUNK, RANK), jnp.float32),
         ),
-        in_specs=[SMEM, VMEM, HBM, HBM, HBM, HBM],
+        in_specs=[VMEM, HBM, HBM, HBM, HBM],
         out_specs=(VMEM,) * 4,
         scratch_shapes=[
             pltpu.VMEM((ZL, TOK, CHUNK), jnp.bfloat16),
@@ -188,7 +190,7 @@
             flops=TOK * RANK * OUT, bytes_accessed=TOK * OUT + 2 * RANK * OUT, transcendentals=0
         ),
         name="own",
-    )(place, in_vmem(turned), *map(in_hbm, (cotangent, basis, m, v)))
+    )(in_vmem(turned), *map(in_hbm, (cotangent, basis, m, v)))
 
 
 def adam_step(gradient, first_moment, second_moment):
@@ -267,11 +269,10 @@
 
 
 def local(inputs, cotangent, projection_basis, first_moment, second_moment):
-    place = jnp.stack([lax.axis_index("fsdp") % 2, lax.axis_index("dp")]).astype(jnp.int32)
-    theirs, turned = first(place, inputs, projection_basis, cotangent)
+    theirs, turned = first(inputs, projection_basis, cotangent)
     got = lax.ppermute(theirs, AXES, SWAP)
     mine, cols, m, v = own(
-        place, turned, cotangent, projection_basis, first_moment, second_moment
+        turned, cotangent, projection_basis, first_moment, second_moment
     )
     both = mine + got
 

time: 95 us -> 91.7 us (0.965)
  the two profiles are of different devices: /device:TPU:2 before, /device:TPU:8 now
where the time goes in v2:
time: 91.7 us; the launch traced here: 91.4 us
  blocking collectives  79.7 us (87%)
  Pallas kernels  6.54 us (7%)
  waiting for transfers between devices  2.05 us (2%)
  starting transfers between devices  1.92 us (2%)
    all_to_all x4, blocking collectives, exchange(): lax.all_to_all(blocks, AXES, 0, 0, axis_index_groups=groups, tiled=True)  79.7 us
    pallas_call x1, Pallas kernels, first(): pl.pallas_call(first_kernel, out_shape=(pltpu.VMEM(HALF, jnp.float32), pl...  3.32 us
    ppermute x1, waiting for transfers between devices, local(): got = lax.ppermute(theirs, AXES, SWAP)  2.05 us
    ppermute x1, starting transfers between devices, local(): got = lax.ppermute(theirs, AXES, SWAP)  1.92 us
    pallas_call x1, Pallas kernels, own(): pl.pallas_call(own_kernel, out_shape=(pltpu.VMEM(HALF, jnp.float32), pltp...  1.88 us
  transfers between devices with their start and end apart: 1, of which 1 were waited for; matrix products, arithmetic and copies ran while one was open for 0% of the time, Pallas kernels for 2%

profile of v2, /device:TPU:8, one launch (start us, length us, event | category | flops | bytes accessed | tf_op | source)
XLA Modules:
  0.0 91.4 jit_solution(17656363607657086277)
XLA Ops:
  0.6 3.3 %first.1 = (f32[2,4,3,32,640]{4,3,2,1,0:T(8,128)S(1)}, bf16[128,128]{1,0:T(8,128)(2,1)S(1)}) custom-call(bf16[128,8192]{1,0:T(8,128)(2,1)} %x_hbm.1, bf16[8192,128]{1,0:T(8,128)(2,1)} %basis_hbm.1, bf16[128,7680]{1,0:T(8,128)(2,1)} %c_hbm.3), custom_call_target="tpu_custom_call" | custom-call | tf_op jit(solution)/shard_map/first/pallas_call | solution.py:140
  4.0 1.9 %collective-permute-start = (f32[2,4,3,32,640]{4,3,2,1,0:T(8,128)S(1)}, f32[2,4,3,32,640]{4,3,2,1,0:T(8,128)S(1)}, u32[]{:S(2)}, u32[]{:S(2)}) collective-permute-start(f32[2,4,3,32,640]{4,3,2,1,0:T(8,128)S(1)} %get-tuple-element.11), channel_id=1, source_target_pairs={{0,64},{64,0},{128,192},{192,128},{256,320},{320,256},{384,448},{4... | collective-permute-start | bytes 5898248 | tf_op jit(solution)/shard_map/ppermute | solution.py:273
  5.9 1.9 %own.1 = (f32[2,4,3,32,640]{4,3,2,1,0:T(8,128)S(1)}, bf16[128,128]{1,0:T(8,128)(2,1)S(1)}, f32[640,128]{1,0:T(8,128)S(1)}, f32[640,128]{1,0:T(8,128)S(1)}) custom-call(bf16[128,128]{1,0:T(8,128)(2,1)S(1)} %get-tuple-element.9.turned, bf16[128,7680]{1,0:T(8,128)(2,1)} %c_hbm.3, bf16[8192,128]{1,0:T(8,128)(2,1)} %basis_hbm.1, f32[640,128]{1,0:T(8,128)} %m_hbm.1, ...), custom_call_target="tpu_custom_call" | custom-call | flops 125829120 | bytes 2949120 | tf_op jit(solution)/shard_map/own/pallas_call | solution.py:173
  7.8 2.0 %collective-permute-done = f32[2,4,3,32,640]{4,3,2,1,0:T(8,128)S(1)} collective-permute-done((f32[2,4,3,32,640]{4,3,2,1,0:T(8,128)S(1)}, f32[2,4,3,32,640]{4,3,2,1,0:T(8,128)S(1)}, u32[]{:S(2)}, u32[]{:S(2)}) %collective-permute-start) | collective-permute-done | bytes 1966112 | tf_op jit(solution)/shard_map/ppermute | solution.py:273
  9.8 0.2 add.3
  10.0 26.5 %all_to_all.20 = f32[8,3,32,640]{3,2,1,0:T(8,128)S(1)} all-to-all(f32[8,3,32,640]{3,2,1,0:T(8,128)S(1)} %bitcast.2), channel_id=1, replica_groups={{17,16,1,0,145,144,129,128},{273,272,257,256,401,400,385,384},{529,528,..., dimensions={0} | all-to-all | bytes 3932160 | tf_op jit(solution)/shard_map/all_to_all | solution.py:79
  36.5 0.1 reduce_sum.18
  36.6 0.1 reshape.13
  36.7 13.4 %all_to_all.21 = f32[8,3,4,640]{3,2,1,0:T(4,128)S(1)} all-to-all(f32[8,3,4,640]{3,2,1,0:T(4,128)S(1)} %copy.8), channel_id=1, replica_groups={{17,18,20,23,33,34,36,39},{16,19,21,22,32,35,37,38},{1,2,4,7,49,50,52,5..., dimensions={0} | all-to-all | bytes 491520 | tf_op jit(solution)/shard_map/all_to_all | solution.py:79
  50.1 24.1 %all_to_all.22.deep = f32[6,4,640]{2,1,0:T(4,128)S(1)} all-to-all(f32[6,4,640]{2,1,0:T(4,128)S(1)} %pad_maximum_fusion), channel_id=1, replica_groups={{0,256,512,8,264,520},{128,384,640,136,392,648},{1,257,513,9,265,521},{..., dimensions={0} | all-to-all | bytes 122880 | tf_op jit(solution)/shard_map/all_to_all | solution.py:79
  74.3 15.8 %all_to_all.23.parts = f32[32,4,640]{2,1,0:T(4,128)S(1)} all-to-all(f32[32,4,640]{2,1,0:T(4,128)S(1)} %spread.1), channel_id=1, replica_groups={{17,18,20,23,33,34,36,39,16,19,21,22,32,35,37,38,1,2,4,7,49,50,52,55,0,..., dimensions={0} | all-to-all | bytes 655360 | tf_op jit(solution)/shard_map/all_to_all | solution.py:79
  90.1 1.3 %last.1 = (f32[640,128]{1,0:T(8,128)}, f32[640,128]{1,0:T(8,128)}, f32[640,128]{1,0:T(8,128)}) custom-call(f32[32,4,640]{2,1,0:T(4,128)S(1)} %all_to_all.23.parts, bf16[128,128]{1,0:T(8,128)(2,1)S(1)} %get-tuple-element.12.cols, f32[640,128]{1,0:T(8,128)S(1)} %get-tuple-element.13.m, f32[640,128]{1,0:T(8,128)S(1)} %get-tuple-element.14.v), custom_call_target="tpu_custom_call" | custom-call | tf_op jit(solution)/shard_map/last/pallas_call | solution.py:255
  (4 shorter events, 0.1 us)
Async XLA Ops:
  4.0 5.9 %collective-permute-start = (f32[2,4,3,32,640]{4,3,2,1,0:T(8,128)S(1)}, f32[2,4,3,32,640]{4,3,2,1,0:T(8,128)S(1)}, u32[]{:S(2)}, u32[]{:S(2)}) collective-permute-start(f32[2,4,3,32,640]{4,3,2,1,0:T(8,128)S(1)} %get-tuple-element.11), channel_id=1, source_target_pairs={{0,64},{64,0},{128,192},{192,128},{256,320},{320,256},{384,448},{4... | collective-permute-start | bytes 5898248 | tf_op jit(solution)/shard_map/ppermute | solution.py:273

commit v3 on v2

--- a/solution.py
+++ b/solution.py
@@ -45,7 +45,7 @@
     for c in CORES
     for px in pairs(X, c, SETS_X[c])
     for py in pairs(Y, c, SETS_Y[c])
-    for pz in pairs(Z, c, EVEN_ODD)
+    for pz in pairs(Z, 1 - c, EVEN_ODD)
 ]
 FAR = [
     [device(x, y, z, c) for x in xs for y in ys]
@@ -198,6 +198,46 @@
     second_new = 0.999 * second_moment + 0.001 * gradient * gradient
     direction = first_new / bias_first / (jnp.sqrt(second_new / bias_second) + 1e-08)
     return (first_new, second_new, direction)
+
+
+def settle_kernel(near, out):
+    for k in range(near.shape[1]):
+        total = near[0, k]
+        for i in range(1, near.shape[0]):
+            total += near[i, k]
+        height = out.shape[2]
+        for r in range(out.shape[0]):
+            out[r, k] = total[r * height : (r + 1) * height]
+
+
+def settle(near):
+    _, chunks, rows, width = near.shape
+    return pl.pallas_call(
+        settle_kernel,
+        out_shape=pltpu.VMEM((8, chunks, rows // 8, width), jnp.float32),
+        in_specs=[VMEM],
+        out_specs=VMEM,
+        name="settle",
+    )(in_vmem(near))
+
+
+def twice_kernel(far, out):
+    for k in range(far.shape[1]):
+        total = far[0, k]
+        for i in range(1, far.shape[0]):
+            total += far[i, k]
+        for h in range(ZH):
+            out[h * ZL // 2 + k] = total
+
+
+def twice(far):
+    return pl.pallas_call(
+        twice_kernel,
+        out_shape=pltpu.VMEM((Z // 2,) + far.shape[2:], jnp.float32),
+        in_specs=[VMEM],
+        out_specs=VMEM,
+        name="twice",
+    )(in_vmem(far))
 
 
 def spread_kernel(deep, out):
@@ -277,10 +317,8 @@
     both = mine + got
 
     near = exchange(both.reshape(8, ZL // 2, RANK // 4, CHUNK), NEAR)
-    near = jnp.sum(near, axis=0).reshape(ZL // 2, 8, RANK // 32, CHUNK)
-    far = exchange(near.transpose(1, 0, 2, 3), FAR)
-    far = jnp.sum(far, axis=0)
-    deep = exchange(jnp.concatenate([far, far], axis=0), DEEP)
+    far = exchange(settle(near), FAR)
+    deep = exchange(twice(far), DEEP)
     whole = exchange(spread(deep), PLANE)
 
     return last(whole, cols, m, v)

time: 91.7 us -> 91.4 us (level)
  no operation moved by 1% of the time
where the time goes in v3:
time: 91.4 us; the launch traced here: 91.1 us
  blocking collectives  79.6 us (87%)
  Pallas kernels  6.66 us (7%)
  waiting for transfers between devices  2.05 us (2%)
  starting transfers between devices  1.92 us (2%)
    all_to_all x4, blocking collectives, exchange(): lax.all_to_all(blocks, AXES, 0, 0, axis_index_groups=groups, tiled=True)  79.6 us
    pallas_call x1, Pallas kernels, first(): pl.pallas_call(first_kernel, out_shape=(pltpu.VMEM(HALF, jnp.float32), pl...  3.32 us
    ppermute x1, waiting for transfers between devices, local(): got = lax.ppermute(theirs, AXES, SWAP)  2.05 us
    ppermute x1, starting transfers between devices, local(): got = lax.ppermute(theirs, AXES, SWAP)  1.92 us
    pallas_call x1, Pallas kernels, own(): pl.pallas_call(own_kernel, out_shape=(pltpu.VMEM(HALF, jnp.float32), pltp...  1.88 us
  transfers between devices with their start and end apart: 1, of which 1 were waited for; matrix products, arithmetic and copies ran while one was open for 0% of the time, Pallas kernels for 2%

profile of v3, /device:TPU:8, one launch (start us, length us, event | category | flops | bytes accessed | tf_op | source)
XLA Modules:
  0.0 91.1 jit_solution(16809754336288209769)
XLA Ops:
  0.6 3.3 %first.1 = (f32[2,4,3,32,640]{4,3,2,1,0:T(8,128)S(1)}, bf16[128,128]{1,0:T(8,128)(2,1)S(1)}) custom-call(bf16[128,8192]{1,0:T(8,128)(2,1)} %x_hbm.1, bf16[8192,128]{1,0:T(8,128)(2,1)} %basis_hbm.1, bf16[128,7680]{1,0:T(8,128)(2,1)} %c_hbm.3), custom_call_target="tpu_custom_call" | custom-call | tf_op jit(solution)/shard_map/first/pallas_call | solution.py:140
  4.0 1.9 %collective-permute-start = (f32[2,4,3,32,640]{4,3,2,1,0:T(8,128)S(1)}, f32[2,4,3,32,640]{4,3,2,1,0:T(8,128)S(1)}, u32[]{:S(2)}, u32[]{:S(2)}) collective-permute-start(f32[2,4,3,32,640]{4,3,2,1,0:T(8,128)S(1)} %get-tuple-element.11), channel_id=1, source_target_pairs={{0,64},{64,0},{128,192},{192,128},{256,320},{320,256},{384,448},{4... | collective-permute-start | bytes 5898248 | tf_op jit(solution)/shard_map/ppermute | solution.py:313
  5.9 1.9 %own.1 = (f32[2,4,3,32,640]{4,3,2,1,0:T(8,128)S(1)}, bf16[128,128]{1,0:T(8,128)(2,1)S(1)}, f32[640,128]{1,0:T(8,128)S(1)}, f32[640,128]{1,0:T(8,128)S(1)}) custom-call(bf16[128,128]{1,0:T(8,128)(2,1)S(1)} %get-tuple-element.9.turned, bf16[128,7680]{1,0:T(8,128)(2,1)} %c_hbm.3, bf16[8192,128]{1,0:T(8,128)(2,1)} %basis_hbm.1, f32[640,128]{1,0:T(8,128)} %m_hbm.1, ...), custom_call_target="tpu_custom_call" | custom-call | flops 125829120 | bytes 2949120 | tf_op jit(solution)/shard_map/own/pallas_call | solution.py:173
  7.8 2.0 %collective-permute-done = f32[2,4,3,32,640]{4,3,2,1,0:T(8,128)S(1)} collective-permute-done((f32[2,4,3,32,640]{4,3,2,1,0:T(8,128)S(1)}, f32[2,4,3,32,640]{4,3,2,1,0:T(8,128)S(1)}, u32[]{:S(2)}, u32[]{:S(2)}) %collective-permute-start) | collective-permute-done | bytes 1966112 | tf_op jit(solution)/shard_map/ppermute | solution.py:313
  9.8 0.2 add.3
  10.0 30.9 %all_to_all.20.near = f32[8,3,32,640]{3,2,1,0:T(8,128)S(1)} all-to-all(f32[8,3,32,640]{3,2,1,0:T(8,128)S(1)} %bitcast.1), channel_id=1, replica_groups={{273,272,257,256,145,144,129,128},{529,528,513,512,401,400,385,384},{25..., dimensions={0} | all-to-all | bytes 3932160 | tf_op jit(solution)/shard_map/all_to_all | solution.py:79
  40.9 0.1 settle.1
  41.0 19.1 %all_to_all.21.far = f32[8,3,4,640]{3,2,1,0:T(4,128)S(1)} all-to-all(f32[8,3,4,640]{3,2,1,0:T(4,128)S(1)} %settle.1), channel_id=1, replica_groups={{17,18,20,23,33,34,36,39},{16,19,21,22,32,35,37,38},{1,2,4,7,49,50,52,5..., dimensions={0} | all-to-all | bytes 491520 | tf_op jit(solution)/shard_map/all_to_all | solution.py:79
  60.2 13.6 %all_to_all.22.deep = f32[6,4,640]{2,1,0:T(4,128)S(1)} all-to-all(f32[6,4,640]{2,1,0:T(4,128)S(1)} %twice.1), channel_id=1, replica_groups={{0,256,512,8,264,520},{128,384,640,136,392,648},{1,257,513,9,265,521},{..., dimensions={0} | all-to-all | bytes 122880 | tf_op jit(solution)/shard_map/all_to_all | solution.py:79
  73.8 16.0 %all_to_all.23.parts = f32[32,4,640]{2,1,0:T(4,128)S(1)} all-to-all(f32[32,4,640]{2,1,0:T(4,128)S(1)} %spread.1), channel_id=1, replica_groups={{17,18,20,23,33,34,36,39,16,19,21,22,32,35,37,38,1,2,4,7,49,50,52,55,0,..., dimensions={0} | all-to-all | bytes 655360 | tf_op jit(solution)/shard_map/all_to_all | solution.py:79
  89.8 1.3 %last.1 = (f32[640,128]{1,0:T(8,128)}, f32[640,128]{1,0:T(8,128)}, f32[640,128]{1,0:T(8,128)}) custom-call(f32[32,4,640]{2,1,0:T(4,128)S(1)} %all_to_all.23.parts, bf16[128,128]{1,0:T(8,128)(2,1)S(1)} %get-tuple-element.12.cols, f32[640,128]{1,0:T(8,128)S(1)} %get-tuple-element.13.m, f32[640,128]{1,0:T(8,128)S(1)} %get-tuple-element.14.v), custom_call_target="tpu_custom_call" | custom-call | tf_op jit(solution)/shard_map/last/pallas_call | solution.py:295
  (2 shorter events, 0.1 us)
Async XLA Ops:
  4.0 5.9 %collective-permute-start = (f32[2,4,3,32,640]{4,3,2,1,0:T(8,128)S(1)}, f32[2,4,3,32,640]{4,3,2,1,0:T(8,128)S(1)}, u32[]{:S(2)}, u32[]{:S(2)}) collective-permute-start(f32[2,4,3,32,640]{4,3,2,1,0:T(8,128)S(1)} %get-tuple-element.11), channel_id=1, source_target_pairs={{0,64},{64,0},{128,192},{192,128},{256,320},{320,256},{384,448},{4... | collective-permute-start | bytes 5898248 | tf_op jit(solution)/shard_map/ppermute | solution.py:313

commit v4 on v3

--- a/solution.py
+++ b/solution.py
@@ -29,7 +29,7 @@
     return tuple(tuple((i + core) % size for i in places) for places in (first, second))
 
 
-SETS_X = [split(X, c, (1, 2), (0, 3)) for c in CORES]
+SETS_X = [((0, 2), (1, 3)), split(X, 1, (1, 2), (0, 3))]
 SETS_Y = [split(Y, c, (1, 2, 4, 7), (0, 3, 5, 6)) for c in CORES]
 
 

time: 91.4 us -> 92.2 us (level)
  no operation moved by 1% of the time
where the time goes in v4:
time: 92.2 us; the launch traced here: 91.9 us
  blocking collectives  80.4 us (87%)
  Pallas kernels  6.66 us (7%)
  waiting for transfers between devices  2.05 us (2%)
  starting transfers between devices  1.92 us (2%)
    all_to_all x4, blocking collectives, exchange(): lax.all_to_all(blocks, AXES, 0, 0, axis_index_groups=groups, tiled=True)  80.4 us
    pallas_call x1, Pallas kernels, first(): pl.pallas_call(first_kernel, out_shape=(pltpu.VMEM(HALF, jnp.float32), pl...  3.32 us
    ppermute x1, waiting for transfers between devices, local(): got = lax.ppermute(theirs, AXES, SWAP)  2.05 us
    ppermute x1, starting transfers between devices, local(): got = lax.ppermute(theirs, AXES, SWAP)  1.92 us
    pallas_call x1, Pallas kernels, own(): pl.pallas_call(own_kernel, out_shape=(pltpu.VMEM(HALF, jnp.float32), pltp...  1.88 us
  transfers between devices with their start and end apart: 1, of which 1 were waited for; matrix products, arithmetic and copies ran while one was open for 0% of the time, Pallas kernels for 2%

profile of v4, /device:TPU:8, one launch (start us, length us, event | category | flops | bytes accessed | tf_op | source)
XLA Modules:
  0.0 91.9 jit_solution(8504767190753615066)
XLA Ops:
  0.6 3.3 %first.1 = (f32[2,4,3,32,640]{4,3,2,1,0:T(8,128)S(1)}, bf16[128,128]{1,0:T(8,128)(2,1)S(1)}) custom-call(bf16[128,8192]{1,0:T(8,128)(2,1)} %x_hbm.1, bf16[8192,128]{1,0:T(8,128)(2,1)} %basis_hbm.1, bf16[128,7680]{1,0:T(8,128)(2,1)} %c_hbm.3), custom_call_target="tpu_custom_call" | custom-call | tf_op jit(solution)/shard_map/first/pallas_call | solution.py:140
  4.0 1.9 %collective-permute-start = (f32[2,4,3,32,640]{4,3,2,1,0:T(8,128)S(1)}, f32[2,4,3,32,640]{4,3,2,1,0:T(8,128)S(1)}, u32[]{:S(2)}, u32[]{:S(2)}) collective-permute-start(f32[2,4,3,32,640]{4,3,2,1,0:T(8,128)S(1)} %get-tuple-element.11), channel_id=1, source_target_pairs={{0,64},{64,0},{128,192},{192,128},{256,320},{320,256},{384,448},{4... | collective-permute-start | bytes 5898248 | tf_op jit(solution)/shard_map/ppermute | solution.py:313
  5.9 1.9 %own.1 = (f32[2,4,3,32,640]{4,3,2,1,0:T(8,128)S(1)}, bf16[128,128]{1,0:T(8,128)(2,1)S(1)}, f32[640,128]{1,0:T(8,128)S(1)}, f32[640,128]{1,0:T(8,128)S(1)}) custom-call(bf16[128,128]{1,0:T(8,128)(2,1)S(1)} %get-tuple-element.9.turned, bf16[128,7680]{1,0:T(8,128)(2,1)} %c_hbm.3, bf16[8192,128]{1,0:T(8,128)(2,1)} %basis_hbm.1, f32[640,128]{1,0:T(8,128)} %m_hbm.1, ...), custom_call_target="tpu_custom_call" | custom-call | flops 125829120 | bytes 2949120 | tf_op jit(solution)/shard_map/own/pallas_call | solution.py:173
  7.8 2.0 %collective-permute-done = f32[2,4,3,32,640]{4,3,2,1,0:T(8,128)S(1)} collective-permute-done((f32[2,4,3,32,640]{4,3,2,1,0:T(8,128)S(1)}, f32[2,4,3,32,640]{4,3,2,1,0:T(8,128)S(1)}, u32[]{:S(2)}, u32[]{:S(2)}) %collective-permute-start) | collective-permute-done | bytes 1966112 | tf_op jit(solution)/shard_map/ppermute | solution.py:313
  9.8 0.2 add.3
  10.0 31.8 %all_to_all.20.near = f32[8,3,32,640]{3,2,1,0:T(8,128)S(1)} all-to-all(f32[8,3,32,640]{3,2,1,0:T(8,128)S(1)} %bitcast.1), channel_id=1, replica_groups={{257,256,273,272,129,128,145,144},{513,512,529,528,385,384,401,400},{9,..., dimensions={0} | all-to-all | bytes 3932160 | tf_op jit(solution)/shard_map/all_to_all | solution.py:79
  41.8 0.1 settle.1
  41.9 19.2 %all_to_all.21.far = f32[8,3,4,640]{3,2,1,0:T(4,128)S(1)} all-to-all(f32[8,3,4,640]{3,2,1,0:T(4,128)S(1)} %settle.1), channel_id=1, replica_groups={{1,2,4,7,33,34,36,39},{0,3,5,6,32,35,37,38},{17,18,20,23,49,50,52,55},{..., dimensions={0} | all-to-all | bytes 491520 | tf_op jit(solution)/shard_map/all_to_all | solution.py:79
  61.2 13.4 %all_to_all.22.deep = f32[6,4,640]{2,1,0:T(4,128)S(1)} all-to-all(f32[6,4,640]{2,1,0:T(4,128)S(1)} %twice.1), channel_id=1, replica_groups={{0,256,512,8,264,520},{128,384,640,136,392,648},{1,257,513,9,265,521},{..., dimensions={0} | all-to-all | bytes 122880 | tf_op jit(solution)/shard_map/all_to_all | solution.py:79
  74.7 15.9 %all_to_all.23.parts = f32[32,4,640]{2,1,0:T(4,128)S(1)} all-to-all(f32[32,4,640]{2,1,0:T(4,128)S(1)} %spread.1), channel_id=1, replica_groups={{1,2,4,7,33,34,36,39,0,3,5,6,32,35,37,38,17,18,20,23,49,50,52,55,16,19,..., dimensions={0} | all-to-all | bytes 655360 | tf_op jit(solution)/shard_map/all_to_all | solution.py:79
  90.5 1.3 %last.1 = (f32[640,128]{1,0:T(8,128)}, f32[640,128]{1,0:T(8,128)}, f32[640,128]{1,0:T(8,128)}) custom-call(f32[32,4,640]{2,1,0:T(4,128)S(1)} %all_to_all.23.parts, bf16[128,128]{1,0:T(8,128)(2,1)S(1)} %get-tuple-element.12.cols, f32[640,128]{1,0:T(8,128)S(1)} %get-tuple-element.13.m, f32[640,128]{1,0:T(8,128)S(1)} %get-tuple-element.14.v), custom_call_target="tpu_custom_call" | custom-call | tf_op jit(solution)/shard_map/last/pallas_call | solution.py:295
  (2 shorter events, 0.1 us)
Async XLA Ops:
  4.0 5.9 %collective-permute-start = (f32[2,4,3,32,640]{4,3,2,1,0:T(8,128)S(1)}, f32[2,4,3,32,640]{4,3,2,1,0:T(8,128)S(1)}, u32[]{:S(2)}, u32[]{:S(2)}) collective-permute-start(f32[2,4,3,32,640]{4,3,2,1,0:T(8,128)S(1)} %get-tuple-element.11), channel_id=1, source_target_pairs={{0,64},{64,0},{128,192},{192,128},{256,320},{320,256},{384,448},{4... | collective-permute-start | bytes 5898248 | tf_op jit(solution)/shard_map/ppermute | solution.py:313

commit v5 on v3

--- a/solution.py
+++ b/solution.py
@@ -45,7 +45,7 @@
     for c in CORES
     for px in pairs(X, c, SETS_X[c])
     for py in pairs(Y, c, SETS_Y[c])
-    for pz in pairs(Z, 1 - c, EVEN_ODD)
+    for pz in pairs(Z, c, EVEN_ODD)
 ]
 FAR = [
     [device(x, y, z, c) for x in xs for y in ys]

time: 91.4 us -> 91.5 us (level)
  no operation moved by 1% of the time
where the time goes in v5:
time: 91.5 us; the launch traced here: 91.2 us
  blocking collectives  79.7 us (87%)
  Pallas kernels  6.66 us (7%)
  waiting for transfers between devices  2.05 us (2%)
  starting transfers between devices  1.92 us (2%)
    all_to_all x4, blocking collectives, exchange(): lax.all_to_all(blocks, AXES, 0, 0, axis_index_groups=groups, tiled=True)  79.7 us
    pallas_call x1, Pallas kernels, first(): pl.pallas_call(first_kernel, out_shape=(pltpu.VMEM(HALF, jnp.float32), pl...  3.32 us
    ppermute x1, waiting for transfers between devices, local(): got = lax.ppermute(theirs, AXES, SWAP)  2.05 us
    ppermute x1, starting transfers between devices, local(): got = lax.ppermute(theirs, AXES, SWAP)  1.92 us
    pallas_call x1, Pallas kernels, own(): pl.pallas_call(own_kernel, out_shape=(pltpu.VMEM(HALF, jnp.float32), pltp...  1.88 us
  transfers between devices with their start and end apart: 1, of which 1 were waited for; matrix products, arithmetic and copies ran while one was open for 0% of the time, Pallas kernels for 2%

profile of v5, /device:TPU:8, one launch (start us, length us, event | category | flops | bytes accessed | tf_op | source)
XLA Modules:
  0.0 91.2 jit_solution(13851001605791660590)
XLA Ops:
  0.6 3.3 %first.1 = (f32[2,4,3,32,640]{4,3,2,1,0:T(8,128)S(1)}, bf16[128,128]{1,0:T(8,128)(2,1)S(1)}) custom-call(bf16[128,8192]{1,0:T(8,128)(2,1)} %x_hbm.1, bf16[8192,128]{1,0:T(8,128)(2,1)} %basis_hbm.1, bf16[128,7680]{1,0:T(8,128)(2,1)} %c_hbm.3), custom_call_target="tpu_custom_call" | custom-call | tf_op jit(solution)/shard_map/first/pallas_call | solution.py:140
  4.0 1.9 %collective-permute-start = (f32[2,4,3,32,640]{4,3,2,1,0:T(8,128)S(1)}, f32[2,4,3,32,640]{4,3,2,1,0:T(8,128)S(1)}, u32[]{:S(2)}, u32[]{:S(2)}) collective-permute-start(f32[2,4,3,32,640]{4,3,2,1,0:T(8,128)S(1)} %get-tuple-element.11), channel_id=1, source_target_pairs={{0,64},{64,0},{128,192},{192,128},{256,320},{320,256},{384,448},{4... | collective-permute-start | bytes 5898248 | tf_op jit(solution)/shard_map/ppermute | solution.py:313
  5.9 1.9 %own.1 = (f32[2,4,3,32,640]{4,3,2,1,0:T(8,128)S(1)}, bf16[128,128]{1,0:T(8,128)(2,1)S(1)}, f32[640,128]{1,0:T(8,128)S(1)}, f32[640,128]{1,0:T(8,128)S(1)}) custom-call(bf16[128,128]{1,0:T(8,128)(2,1)S(1)} %get-tuple-element.9.turned, bf16[128,7680]{1,0:T(8,128)(2,1)} %c_hbm.3, bf16[8192,128]{1,0:T(8,128)(2,1)} %basis_hbm.1, f32[640,128]{1,0:T(8,128)} %m_hbm.1, ...), custom_call_target="tpu_custom_call" | custom-call | flops 125829120 | bytes 2949120 | tf_op jit(solution)/shard_map/own/pallas_call | solution.py:173
  7.8 2.0 %collective-permute-done = f32[2,4,3,32,640]{4,3,2,1,0:T(8,128)S(1)} collective-permute-done((f32[2,4,3,32,640]{4,3,2,1,0:T(8,128)S(1)}, f32[2,4,3,32,640]{4,3,2,1,0:T(8,128)S(1)}, u32[]{:S(2)}, u32[]{:S(2)}) %collective-permute-start) | collective-permute-done | bytes 1966112 | tf_op jit(solution)/shard_map/ppermute | solution.py:313
  9.8 0.2 add.3
  10.0 26.5 %all_to_all.20.near = f32[8,3,32,640]{3,2,1,0:T(8,128)S(1)} all-to-all(f32[8,3,32,640]{3,2,1,0:T(8,128)S(1)} %bitcast.1), channel_id=1, replica_groups={{17,16,1,0,145,144,129,128},{273,272,257,256,401,400,385,384},{529,528,..., dimensions={0} | all-to-all | bytes 3932160 | tf_op jit(solution)/shard_map/all_to_all | solution.py:79
  36.5 0.1 settle.1
  36.6 13.4 %all_to_all.21.far = f32[8,3,4,640]{3,2,1,0:T(4,128)S(1)} all-to-all(f32[8,3,4,640]{3,2,1,0:T(4,128)S(1)} %settle.1), channel_id=1, replica_groups={{17,18,20,23,33,34,36,39},{16,19,21,22,32,35,37,38},{1,2,4,7,49,50,52,5..., dimensions={0} | all-to-all | bytes 491520 | tf_op jit(solution)/shard_map/all_to_all | solution.py:79
  50.0 24.1 %all_to_all.22.deep = f32[6,4,640]{2,1,0:T(4,128)S(1)} all-to-all(f32[6,4,640]{2,1,0:T(4,128)S(1)} %twice.1), channel_id=1, replica_groups={{0,256,512,8,264,520},{128,384,640,136,392,648},{1,257,513,9,265,521},{..., dimensions={0} | all-to-all | bytes 122880 | tf_op jit(solution)/shard_map/all_to_all | solution.py:79
  74.1 15.8 %all_to_all.23.parts = f32[32,4,640]{2,1,0:T(4,128)S(1)} all-to-all(f32[32,4,640]{2,1,0:T(4,128)S(1)} %spread.1), channel_id=1, replica_groups={{17,18,20,23,33,34,36,39,16,19,21,22,32,35,37,38,1,2,4,7,49,50,52,55,0,..., dimensions={0} | all-to-all | bytes 655360 | tf_op jit(solution)/shard_map/all_to_all | solution.py:79
  89.9 1.3 %last.1 = (f32[640,128]{1,0:T(8,128)}, f32[640,128]{1,0:T(8,128)}, f32[640,128]{1,0:T(8,128)}) custom-call(f32[32,4,640]{2,1,0:T(4,128)S(1)} %all_to_all.23.parts, bf16[128,128]{1,0:T(8,128)(2,1)S(1)} %get-tuple-element.12.cols, f32[640,128]{1,0:T(8,128)S(1)} %get-tuple-element.13.m, f32[640,128]{1,0:T(8,128)S(1)} %get-tuple-element.14.v), custom_call_target="tpu_custom_call" | custom-call | tf_op jit(solution)/shard_map/last/pallas_call | solution.py:295
  (2 shorter events, 0.1 us)
Async XLA Ops:
  4.0 5.9 %collective-permute-start = (f32[2,4,3,32,640]{4,3,2,1,0:T(8,128)S(1)}, f32[2,4,3,32,640]{4,3,2,1,0:T(8,128)S(1)}, u32[]{:S(2)}, u32[]{:S(2)}) collective-permute-start(f32[2,4,3,32,640]{4,3,2,1,0:T(8,128)S(1)} %get-tuple-element.11), channel_id=1, source_target_pairs={{0,64},{64,0},{128,192},{192,128},{256,320},{320,256},{384,448},{4... | collective-permute-start | bytes 5898248 | tf_op jit(solution)/shard_map/ppermute | solution.py:313
